TPU v7x, 32 devices: a whole 2x2x4 slice. The times are simulated.
32 devices in a mesh: dp: 2 (over y), expert: 16 (over z, x, core).
Axes of the slice: x: 2, y: 2, z: 4, core: 2. Of those that a mesh axis runs over, the one named last changes fastest.
Arguments:
- tokens: bfloat16 [1024, 2048], P(('dp', 'expert')), may hold values from -6 to 6
- routes: int32 [1024, 8], P(('dp', 'expert')), may hold values from 0 to 15, all different within a row; in each aligned block of 32 rows (0 to 31, 32 to 63, ...) at most 32 rows name the same one
- cotangent: bfloat16 [1024, 2048], P(('dp', 'expert')), may hold values from -6 to 6
- router_weight: bfloat16 [2048, 16], replicated, may hold values from -0.375 to 0.375
- gate_weight: bfloat16 [16, 2048, 768], P('expert'), may hold values from -0.125 to 0.125
- up_weight: bfloat16 [16, 2048, 768], P('expert'), may hold values from -0.125 to 0.125
- down_weight: bfloat16 [16, 768, 2048], P('expert'), may hold values from -0.21875 to 0.21875
Outputs:
- layer_out: bfloat16 [1024, 2048], P(('dp', 'expert'))
- token_grad: bfloat16 [1024, 2048], P(('dp', 'expert'))
- gate_grad: bfloat16 [16, 2048, 768], P('expert', 'dp')
- up_grad: bfloat16 [16, 2048, 768], P('expert', 'dp')
- down_grad: bfloat16 [16, 768, 2048], P('expert', None, 'dp')
- router_grad: float32 [2048, 16], replicated
Inputs may be any that keep to these rules, and one draw needn't show every extreme that they name: `routes`: each row names 8 different experts. Among the 32 rows of one device no expert is named by more than 32 rows, and in some device's rows an expert is named by exactly 32 rows.
All inputs are finite; a program needn't handle non-finite values.
Results may differ from a plain program's by a relative error of at most 0.0061.
Values may be sent and summed in bfloat16 or wider, within the bound.
A program may use at most 128 MiB of HBM per device.

v0:
```python
import jax
import jax.numpy as jnp
from jax import lax
from jax.sharding import PartitionSpec as P


def silu_parts(gate_act):
    sigmoid_value = jax.nn.sigmoid(gate_act)
    act_value = gate_act * sigmoid_value
    act_slope = sigmoid_value * (1.0 + gate_act * (1.0 - sigmoid_value))
    return (act_value, act_slope)


def expert_forward(arrived, gate_weight, up_weight, down_weight):
    gate_act = jnp.einsum(
        "sjcd,jdf->sjcf", arrived, gate_weight, preferred_element_type=jnp.float32
    )
    up_act = jnp.einsum("sjcd,jdf->sjcf", arrived, up_weight, preferred_element_type=jnp.float32)
    act_value, act_slope = silu_parts(gate_act)
    hidden = (act_value * up_act).astype(jnp.bfloat16)
    expert_out = jnp.einsum(
        "sjcf,jfd->sjcd", hidden, down_weight, preferred_element_type=jnp.float32
    ).astype(jnp.bfloat16)
    return (expert_out, (up_act, act_value, act_slope, hidden))


def expert_backward(arrived_grads, stored, gate_weight, up_weight, down_weight):
    up_act, act_value, act_slope, hidden = stored
    hidden_grad = jnp.einsum(
        "sjcd,jfd->sjcf", arrived_grads, down_weight, preferred_element_type=jnp.float32
    )
    gate_part = (hidden_grad * up_act * act_slope).astype(jnp.bfloat16)
    up_part = (hidden_grad * act_value).astype(jnp.bfloat16)
    input_grad = (
        jnp.einsum("sjcf,jdf->sjcd", gate_part, gate_weight, preferred_element_type=jnp.float32)
        + jnp.einsum("sjcf,jdf->sjcd", up_part, up_weight, preferred_element_type=jnp.float32)
    ).astype(jnp.bfloat16)
    return (input_grad, gate_part, up_part)


def local(tokens, routes, cotangent, router_weight, gate_weight, up_weight, down_weight):
    tok_rows, top_count = routes.shape
    model_width = tokens.shape[1]
    expert_count = router_weight.shape[1]
    local_count = gate_weight.shape[0]
    group_size = lax.axis_size("expert")
    capacity = min(tok_rows, 2 * tok_rows * top_count // expert_count)
    slot_total = expert_count * capacity
    buffer_shape = (group_size, local_count, capacity, model_width)
    logits = jnp.dot(tokens, router_weight, preferred_element_type=jnp.float32)
    exp_logits = jnp.exp(logits)
    probability = exp_logits / jnp.sum(exp_logits, axis=1, keepdims=True)
    chosen = (
        routes[:, :, None] == jnp.arange(expert_count, dtype=jnp.int32)[None, None, :]
    ).astype(jnp.int32)
    chosen_float = chosen.astype(jnp.float32)
    selected = jnp.sum(chosen_float * probability[:, None, :], axis=2)
    sel_total = jnp.sum(selected, axis=1, keepdims=True)
    combine = selected / sel_total
    per_token = jnp.sum(chosen, axis=1)
    earlier = jnp.cumsum(per_token, axis=0) - per_token
    slot_ids = jnp.sum(chosen * earlier[:, None, :], axis=2)
    flat_slot = routes * capacity + slot_ids
    match_map = (
        flat_slot[:, :, None] == jnp.arange(slot_total, dtype=jnp.int32)[None, None, :]
    ).astype(jnp.float32)
    presence = jnp.sum(match_map, axis=1)
    weight_map = jnp.sum(match_map * combine[:, :, None], axis=1)
    send_rows = (
        jnp.einsum(
            "tr,td->rd", presence.astype(jnp.bfloat16), tokens, preferred_element_type=jnp.float32
        )
        .astype(jnp.bfloat16)
        .reshape(buffer_shape)
    )
    send_grads = (
        jnp.einsum(
            "tr,td->rd", weight_map, cotangent.astype(jnp.float32), precision=lax.Precision.HIGHEST
        )
        .astype(jnp.bfloat16)
        .reshape(buffer_shape)
    )
    arrived = lax.all_to_all(send_rows, "expert", split_axis=0, concat_axis=0, tiled=True)
    expert_out, stored = expert_forward(arrived, gate_weight, up_weight, down_weight)
    returned = lax.all_to_all(expert_out, "expert", split_axis=0, concat_axis=0, tiled=True)
    arrived_grads = lax.all_to_all(send_grads, "expert", split_axis=0, concat_axis=0, tiled=True)
    input_grad, gate_part, up_part = expert_backward(
        arrived_grads, stored, gate_weight, up_weight, down_weight
    )
    returned_grads = lax.all_to_all(input_grad, "expert", split_axis=0, concat_axis=0, tiled=True)
    hidden = stored[3]
    gate_term = jnp.einsum("sjcd,sjcf->jdf", arrived, gate_part, preferred_element_type=jnp.float32)
    up_term = jnp.einsum("sjcd,sjcf->jdf", arrived, up_part, preferred_element_type=jnp.float32)
    down_term = jnp.einsum(
        "sjcf,sjcd->jfd", hidden, arrived_grads, preferred_element_type=jnp.float32
    )
    gate_sum, up_sum, down_sum = (
        lax.psum_scatter(gate_term, "dp", scatter_dimension=1, tiled=True),
        lax.psum_scatter(up_term, "dp", scatter_dimension=1, tiled=True),
        lax.psum_scatter(down_term, "dp", scatter_dimension=2, tiled=True),
    )
    gate_grad = gate_sum.astype(jnp.bfloat16)
    up_grad = up_sum.astype(jnp.bfloat16)
    down_grad = down_sum.astype(jnp.bfloat16)
    flat_index = flat_slot.reshape(-1)
    out_sel = jnp.take(returned.reshape(slot_total, model_width), flat_index, axis=0).reshape(
        tok_rows, top_count, model_width
    )
    grad_sel = jnp.take(
        returned_grads.reshape(slot_total, model_width), flat_index, axis=0
    ).reshape(tok_rows, top_count, model_width)
    layer_out = jnp.sum(combine[:, :, None] * out_sel.astype(jnp.float32), axis=1).astype(
        jnp.bfloat16
    )
    comb_grad = jnp.einsum("tkd,td->tk", out_sel, cotangent, preferred_element_type=jnp.float32)
    sel_grad = (comb_grad - jnp.sum(combine * comb_grad, axis=1, keepdims=True)) / sel_total
    prob_grad = jnp.sum(chosen_float * sel_grad[:, :, None], axis=1)
    logit_grad = probability * (prob_grad - jnp.sum(probability * prob_grad, axis=1, keepdims=True))
    router_term = jnp.einsum(
        "td,te->de", tokens.astype(jnp.float32), logit_grad, precision=lax.Precision.HIGHEST
    )
    router_grad = lax.psum(router_term, ("dp", "expert"))
    router_back = jnp.einsum(
        "te,de->td", logit_grad, router_weight.astype(jnp.float32), precision=lax.Precision.HIGHEST
    )
    token_grad = (jnp.sum(grad_sel.astype(jnp.float32), axis=1) + router_back).astype(jnp.bfloat16)
    return (layer_out, token_grad, gate_grad, up_grad, down_grad, router_grad)


def solution(mesh):
    return jax.shard_map(
        local,
        mesh=mesh,
        in_specs=(
            P(("dp", "expert"), None),
            P(("dp", "expert"), None),
            P(("dp", "expert"), None),
            P(),
            P("expert", None, None),
            P("expert", None, None),
            P("expert", None, None),
        ),
        out_specs=(
            P(("dp", "expert"), None),
            P(("dp", "expert"), None),
            P("expert", "dp", None),
            P("expert", "dp", None),
            P("expert", None, "dp"),
            P(),
        ),
        check_vma=False,
    )
```

profile of v0, /device:TPU:0, one launch (start us, length us, event | category | flops | bytes accessed | tf_op | source)
XLA Modules:
  0.0 455.1 jit_solution(14684139448227573478)
XLA Ops:
  8.9 1.1 fusion.55
  12.9 4.0 convolution_convert_fusion
  16.9 7.5 %all-to-all-start.2 = ((bf16[16,1,32,2048]{3,2,1,0:T(8,128)(2,1)}), bf16[16,1,32,2048]{3,2,1,0:T(8,128)(2,1)}, u32[]{:S(2)}, u32[]{:S(2)}) async-start(bf16[16,1,32,2048]{3,2,1,0:T(8,128)(2,1)} %bitcast.170), calls=%async_computation.2 | async-start | bytes 4194304 | tf_op jit(solution)/shard_map/all_to_all | solution.py:86
  24.5 2.1 convolution_convert_fusion.1
  26.6 39.1 %all-to-all-done.2 = bf16[16,1,32,2048]{3,2,1,0:T(8,128)(2,1)} async-done(((bf16[16,1,32,2048]{3,2,1,0:T(8,128)(2,1)}), bf16[16,1,32,2048]{3,2,1,0:T(8,128)(2,1)}, u32[]{:S(2)}, u32[]{:S(2)}) %all-to-all-start.2) | async-done | bytes 2097184 | tf_op jit(solution)/shard_map/all_to_all | solution.py:86
  65.7 11.3 %all-to-all-start = ((bf16[16,1,32,2048]{3,2,1,0:T(8,128)(2,1)}), bf16[16,1,32,2048]{3,2,1,0:T(8,128)(2,1)}, u32[]{:S(2)}, u32[]{:S(2)}) async-start(bf16[16,1,32,2048]{3,2,1,0:T(8,128)(2,1)} %bitcast.169), calls=%async_computation | async-start | bytes 4194304 | tf_op jit(solution)/shard_map/all_to_all | solution.py:83
  77.0 5.5 %fusion = f32[16,32,768]{2,1,0:T(8,128)} fusion(bf16[1,768,2048]{2,1,0:T(8,128)(2,1)} %param.15, bf16[16,1,32,2048]{3,2,1,0:T(8,128)(2,1)} %all-to-all-done.2), kind=kOutput, calls=%fused_computation.6 | convolution fusion | flops 1610612736 | bytes 6815744 | tf_op jit(solution)/shard_map/sjcd,jfd->sjcf/dot_general | solution.py:29
  82.5 35.6 %all-to-all-done = bf16[16,1,32,2048]{3,2,1,0:T(8,128)(2,1)} async-done(((bf16[16,1,32,2048]{3,2,1,0:T(8,128)(2,1)}), bf16[16,1,32,2048]{3,2,1,0:T(8,128)(2,1)}, u32[]{:S(2)}, u32[]{:S(2)}) %all-to-all-start) | async-done | bytes 2097184 | tf_op jit(solution)/shard_map/all_to_all | solution.py:83
  118.1 4.4 fusion.6
  122.5 5.1 %fusion.41 = (bf16[16,32,768]{2,1,0:T(8,128)(2,1)S(1)}, bf16[16,1,32,768]{3,2,0,1:T(8,128)(2,1)}, bf16[16,32,768]{2,1,0:T(8,128)(2,1)}) fusion(f32[16,32,768]{2,1,0:T(8,128)S(1)} %fusion.6, f32[16,32,768]{2,1,0:T(8,128)S(1)} %copy-done.6, bf16[1,2048,768]{2,1,0:T(8,128)(2,1)S(1)} %copy-done, bf16[16,1,32,2048]{3,2,1,0:T(8,128)(2,1)} %all-to-all-done), kind=kOutput, calls=%fused_computation.53 | convolution fusion | flops 1616510976 | bytes 10747904 | tf_op jit(solution)/shard_map/sjcd,jdf->sjcf/dot_general | solution.py:15
  128.5 6.1 %convolution_bitcast_fusion = f32[1,768,2048]{2,1,0:T(8,128)} fusion(bf16[16,32,768]{2,1,0:T(8,128)(2,1)S(1)} %get-tuple-element.13, bf16[16,1,32,2048]{3,2,1,0:T(8,128)(2,1)} %all-to-all-done.2), kind=kOutput, calls=%fused_computation.3 | convolution fusion | flops 1610612736 | bytes 9175040 | tf_op jit(solution)/shard_map/sjcf,sjcd->jfd/dot_general | solution.py:94
  134.7 6.3 %convolution_bitcast_fusion.2 = f32[1,2048,768]{2,1,0:T(8,128)} fusion(bf16[16,1,32,2048]{3,2,1,0:T(8,128)(2,1)} %all-to-all-done, bf16[16,1,32,768]{3,2,0,1:T(8,128)(2,1)} %get-tuple-element.14), kind=kOutput, calls=%fused_computation.5 | convolution fusion | flops 1610612736 | bytes 9175040 | tf_op jit(solution)/shard_map/sjcd,sjcf->jdf/dot_general | solution.py:92
  141.2 6.3 %convolution_bitcast_fusion.1 = f32[1,2048,768]{2,1,0:T(8,128)} fusion(bf16[16,32,768]{2,1,0:T(8,128)(2,1)} %get-tuple-element.15, bf16[16,1,32,2048]{3,2,1,0:T(8,128)(2,1)} %all-to-all-done), kind=kOutput, calls=%fused_computation.4 | convolution fusion | flops 1610612736 | bytes 9175040 | tf_op jit(solution)/shard_map/sjcd,sjcf->jdf/dot_general | solution.py:93
  147.5 5.6 %fusion.17 = bf16[16,1,32,2048]{3,2,1,0:T(8,128)(2,1)} fusion(bf16[16,32,768]{2,1,0:T(8,128)(2,1)} %copy-done.7, bf16[1,768,2048]{2,1,0:T(8,128)(2,1)} %param.15), kind=kOutput, calls=%fused_computation.21 | convolution fusion | flops 1611661312 | bytes 6029312 | tf_op jit(solution)/shard_map/sjcf,jfd->sjcd/dot_general | solution.py:21
  153.1 11.6 %all-to-all-start.1 = ((bf16[16,1,32,2048]{3,2,1,0:T(8,128)(2,1)}), bf16[16,1,32,2048]{3,2,1,0:T(8,128)(2,1)}, u32[]{:S(2)}, u32[]{:S(2)}) async-start(bf16[16,1,32,2048]{3,2,1,0:T(8,128)(2,1)} %fusion.17), calls=%async_computation.1 | async-start | bytes 4194304 | tf_op jit(solution)/shard_map/all_to_all | solution.py:85
  164.8 4.0 fusion.4
  168.8 3.1 fusion.20
  171.9 34.0 %all-to-all-done.1 = bf16[16,1,32,2048]{3,2,1,0:T(8,128)(2,1)} async-done(((bf16[16,1,32,2048]{3,2,1,0:T(8,128)(2,1)}), bf16[16,1,32,2048]{3,2,1,0:T(8,128)(2,1)}, u32[]{:S(2)}, u32[]{:S(2)}) %all-to-all-start.1) | async-done | bytes 2097184 | tf_op jit(solution)/shard_map/all_to_all | solution.py:85
  205.9 11.3 %all-to-all-start.3 = ((bf16[16,1,32,2048]{3,2,1,0:T(8,128)(2,1)}), bf16[16,1,32,2048]{3,2,1,0:T(8,128)(2,1)}, u32[]{:S(2)}, u32[]{:S(2)}) async-start(bf16[16,1,32,2048]{3,2,1,0:T(8,128)(2,1)} %fusion.20), calls=%async_computation.3 | async-start | bytes 4194304 | tf_op jit(solution)/shard_map/all_to_all | solution.py:90
  217.4 5.3 %gather_fusion = bf16[256,2048]{1,0:T(8,128)(2,1)} fusion(bf16[512,2048]{1,0:T(8,128)(2,1)} %bitcast.22, s32[1024]{0:T(1024)S(1)} %pad_clamp_fusion), kind=kCustom, calls=%fused_computation.clone | custom fusion | bytes 2098176 | tf_op jit(solution)/shard_map/jit(_take)/gather | solution.py:106
  222.7 2.1 fusion.39
  224.9 33.4 %all-to-all-done.3 = bf16[16,1,32,2048]{3,2,1,0:T(8,128)(2,1)} async-done(((bf16[16,1,32,2048]{3,2,1,0:T(8,128)(2,1)}), bf16[16,1,32,2048]{3,2,1,0:T(8,128)(2,1)}, u32[]{:S(2)}, u32[]{:S(2)}) %all-to-all-start.3) | async-done | bytes 2097184 | tf_op jit(solution)/shard_map/all_to_all | solution.py:90
  258.3 5.2 %gather_fusion.1 = bf16[256,2048]{1,0:T(8,128)(2,1)} fusion(bf16[512,2048]{1,0:T(8,128)(2,1)} %bitcast.40, s32[1024]{0:T(1024)S(1)} %pad_clamp_fusion), kind=kCustom, calls=%fused_computation.1.clone | custom fusion | bytes 2098176 | tf_op jit(solution)/shard_map/jit(_take)/gather | solution.py:109
  264.5 4.0 convert_reduce_fusion
  268.5 1.0 fusion.23
  269.5 3.3 convert_element_type.102
  272.7 25.2 %reduce-scatter.4.cloned.1.call-done = f32[1,1024,768]{2,1,0:T(8,128)} async-done(((f32[1,2048,768]{2,1,0:T(8,128)}), f32[1,1024,768]{2,1,0:T(8,128)}) %reduce-scatter.4.cloned.1.call-update) | async-done | bytes 3145744 | tf_op jit(solution)/shard_map/reduce_scatter | solution.py:98
  297.9 3.2 convert_element_type.100
  301.1 76.4 %reduce-scatter.6.cloned.1.call-done = f32[1,1024,768]{2,1,0:T(8,128)} async-done(((f32[1,2048,768]{2,1,0:T(8,128)}), f32[1,1024,768]{2,1,0:T(8,128)}) %reduce-scatter.6.cloned.1.call-update) | async-done | bytes 3145744 | tf_op jit(solution)/shard_map/reduce_scatter | solution.py:99
  377.6 3.2 convert_element_type.101
  380.8 65.6 %all-reduce.2.cloned.1.call-done = f32[2048,16]{0,1:T(8,128)} async-done(((f32[2048,16]{0,1:T(8,128)}), f32[2048,16]{0,1:T(8,128)}) %all-reduce.2.cloned.1.call-update) | async-done | bytes 131088 | tf_op jit(solution)/shard_map/psum | solution.py:122
  446.4 1.6 copy.44
  (48 shorter events, 6.2 us)
Async XLA Ops:
  8.0 114.5 %copy-start = (bf16[1,2048,768]{2,1,0:T(8,128)(2,1)S(1)}, bf16[1,2048,768]{2,1,0:T(8,128)(2,1)}, u32[]{:S(2)}) copy-start(bf16[1,2048,768]{2,1,0:T(8,128)(2,1)} %param.13) | copy-start | bytes 9437188
  16.9 7.6 %copy-start.1 = (bf16[32,2048]{1,0:T(8,128)(2,1)S(1)}, bf16[32,2048]{1,0:T(8,128)(2,1)}, u32[]{:S(2)}) copy-start(bf16[32,2048]{1,0:T(8,128)(2,1)} %param.9) | copy-start | bytes 393220
  16.9 48.7 %all-to-all-start.2 = ((bf16[16,1,32,2048]{3,2,1,0:T(8,128)(2,1)}), bf16[16,1,32,2048]{3,2,1,0:T(8,128)(2,1)}, u32[]{:S(2)}, u32[]{:S(2)}) async-start(bf16[16,1,32,2048]{3,2,1,0:T(8,128)(2,1)} %bitcast.170), calls=%async_computation.2 | async-start | bytes 4194304 | tf_op jit(solution)/shard_map/all_to_all | solution.py:86
  65.7 52.4 %all-to-all-start = ((bf16[16,1,32,2048]{3,2,1,0:T(8,128)(2,1)}), bf16[16,1,32,2048]{3,2,1,0:T(8,128)(2,1)}, u32[]{:S(2)}, u32[]{:S(2)}) async-start(bf16[16,1,32,2048]{3,2,1,0:T(8,128)(2,1)} %bitcast.169), calls=%async_computation | async-start | bytes 4194304 | tf_op jit(solution)/shard_map/all_to_all | solution.py:83
  76.9 192.5 %reduce-scatter.8.cloned.1.call-start = ((), (), s32[]{:S(2)}) async-start(), calls=%async_computation.9 | async-start | bytes 9437184 | tf_op jit(solution)/shard_map/reduce_scatter | solution.py:100
  118.1 4.4 copy-start.6
  127.6 0.9 copy-start.7
  134.6 163.3 %reduce-scatter.4.cloned.1.call-start = ((), (), s32[]{:S(2)}) async-start(), calls=%async_computation.7 | async-start | bytes 9437184 | tf_op jit(solution)/shard_map/reduce_scatter | solution.py:98
  141.0 236.6 %reduce-scatter.6.cloned.1.call-start = ((), (), s32[]{:S(2)}) async-start(), calls=%async_computation.8 | async-start | bytes 9437184 | tf_op jit(solution)/shard_map/reduce_scatter | solution.py:99
  153.1 52.8 %all-to-all-start.1 = ((bf16[16,1,32,2048]{3,2,1,0:T(8,128)(2,1)}), bf16[16,1,32,2048]{3,2,1,0:T(8,128)(2,1)}, u32[]{:S(2)}, u32[]{:S(2)}) async-start(bf16[16,1,32,2048]{3,2,1,0:T(8,128)(2,1)} %fusion.17), calls=%async_computation.1 | async-start | bytes 4194304 | tf_op jit(solution)/shard_map/all_to_all | solution.py:85
  164.7 4.0 copy-start.5
  205.9 52.4 %all-to-all-start.3 = ((bf16[16,1,32,2048]{3,2,1,0:T(8,128)(2,1)}), bf16[16,1,32,2048]{3,2,1,0:T(8,128)(2,1)}, u32[]{:S(2)}, u32[]{:S(2)}) async-start(bf16[16,1,32,2048]{3,2,1,0:T(8,128)(2,1)} %fusion.20), calls=%async_computation.3 | async-start | bytes 4194304 | tf_op jit(solution)/shard_map/all_to_all | solution.py:90
  217.2 229.2 %all-reduce.2.cloned.1.call-start = ((), (), s32[]{:S(2)}) async-start(), calls=%async_computation.10 | async-start | bytes 262144 | tf_op jit(solution)/shard_map/psum | solution.py:122
  217.4 5.4 %copy-start.3 = (bf16[32,2048]{1,0:T(8,128)(2,1)S(1)}, bf16[32,2048]{1,0:T(8,128)(2,1)}, u32[]{:S(2)}) copy-start(bf16[32,2048]{1,0:T(8,128)(2,1)} %param.11) | copy-start | bytes 393220
  258.3 5.2 %copy-start.4 = (s32[32,8]{0,1:T(8,128)S(1)}, s32[32,8]{0,1:T(8,128)}, u32[]{:S(2)}) copy-start(s32[32,8]{0,1:T(8,128)} %param.10) | copy-start | bytes 3076
  263.5 4.9 %copy-start.2 = (bf16[2048,16]{0,1:T(8,128)(2,1)S(1)}, bf16[2048,16]{0,1:T(8,128)(2,1)}, u32[]{:S(2)}) copy-start(bf16[2048,16]{0,1:T(8,128)(2,1)} %param.12) | copy-start | bytes 196612
Sparse Core Ops, SparseCore 0:
  134.7 83.5 reduce-scatter.7
  220.8 77.0 reduce-scatter.3
  300.2 77.2 reduce-scatter.5
Sparse Core Ops, SparseCore 1:
  268.6 177.8 all-reduce.1
where the time goes:
time: 456 us; the launch traced here: 455 us
  waiting for transfers between devices  309 us (68%)
  matrix products  57.6 us (13%)
  starting transfers between devices  42 us (9%)
  other arithmetic  17.2 us (4%)
  between operations  15.4 us (3%)
  local copies, waits for them, and re-layouts  13.5 us (3%)
    reduce_scatter x1, waiting for transfers between devices, local(): lax.psum_scatter(up_term, 'dp', scatter_dimension=1, tiled=True)  76.4 us
    psum x1, waiting for transfers between devices, local(): router_grad = lax.psum(router_term, ('dp', 'expert'))  65.6 us
    all_to_all x1, waiting for transfers between devices, local(): lax.all_to_all(send_grads, 'expert', split_axis=0, concat_axis=0, tiled=T...  39.1 us
    all_to_all x1, waiting for transfers between devices, local(): lax.all_to_all(send_rows, 'expert', split_axis=0, concat_axis=0, tiled=True)  35.6 us
    all_to_all x1, waiting for transfers between devices, local(): lax.all_to_all(expert_out, 'expert', split_axis=0, concat_axis=0, tiled=T...  34 us
    all_to_all x1, waiting for transfers between devices, local(): lax.all_to_all(input_grad, 'expert', split_axis=0, concat_axis=0, tiled=T...  33.4 us
    reduce_scatter x1, waiting for transfers between devices, local(): lax.psum_scatter(gate_term, 'dp', scatter_dimension=1, tiled=True)  25.2 us
    all_to_all x1, starting transfers between devices, local(): lax.all_to_all(expert_out, 'expert', split_axis=0, concat_axis=0, tiled=T...  11.6 us
  transfers between devices with their start and end apart: 8, of which 7 were waited for; matrix products, arithmetic and copies ran while one was open for 13% of the time, Pallas kernels for 0%

commit v1 on v0

--- a/solution.py
+++ b/solution.py
@@ -119,7 +119,7 @@
     router_term = jnp.einsum(
         "td,te->de", tokens.astype(jnp.float32), logit_grad, precision=lax.Precision.HIGHEST
     )
-    router_grad = lax.psum(router_term, ("dp", "expert"))
+    router_grad = lax.psum(lax.psum(router_term, "expert"), "dp")
     router_back = jnp.einsum(
         "te,de->td", logit_grad, router_weight.astype(jnp.float32), precision=lax.Precision.HIGHEST
     )

time: 456 us -> 475 us (1.042)
  blocking collectives: 0 us -> 59.9 us
  waiting for transfers between devices: 309 us -> 282 us
  starting transfers between devices: 42 us -> 30.5 us
    all_to_all x0 -> x1, blocking collectives: none -> 59.9 us  [local(): lax.all_to_all(input_grad, 'expert', split_axis=0, concat_axis=0, tiled=T...]
    reduce_scatter x1, waiting for transfers between devices: 25.2 us -> 66.6 us  [local(): lax.psum_scatter(gate_term, 'dp', scatter_dimension=1, tiled=True)]
    psum x1 -> x2, waiting for transfers between devices: 65.6 us -> 24.3 us  [local(): router_grad = lax.psum(lax.psum(router_term, 'expert'), 'dp')]
    all_to_all x1 -> x0, waiting for transfers between devices: 33.4 us -> none  [local(): lax.all_to_all(input_grad, 'expert', split_axis=0, concat_axis=0, tiled=T...]
    all_to_all x1 -> x0, starting transfers between devices: 11.3 us -> none  [local(): lax.all_to_all(input_grad, 'expert', split_axis=0, concat_axis=0, tiled=T...]
    all_to_all x1, waiting for transfers between devices: 34 us -> 40.8 us  [local(): lax.all_to_all(expert_out, 'expert', split_axis=0, concat_axis=0, tiled=T...]
  transfers between devices with their start and end apart: 8 -> 8, of which waited for: 7 -> 7; matrix products, arithmetic and copies ran while one was open for 13% -> 11% of each run, Pallas kernels for 0% -> 0%
where the time goes in v1:
time: 475 us; the launch traced here: 474 us
  waiting for transfers between devices  282 us (59%)
  blocking collectives  59.9 us (13%)
  matrix products  54.5 us (11%)
  starting transfers between devices  30.5 us (6%)
  other arithmetic  17.2 us (4%)
  between operations  15.9 us (3%)
  local copies, waits for them, and re-layouts  13.4 us (3%)
    reduce_scatter x1, waiting for transfers between devices, local(): lax.psum_scatter(up_term, 'dp', scatter_dimension=1, tiled=True)  76 us
    reduce_scatter x1, waiting for transfers between devices, local(): lax.psum_scatter(gate_term, 'dp', scatter_dimension=1, tiled=True)  66.6 us
    all_to_all x1, blocking collectives, local(): lax.all_to_all(input_grad, 'expert', split_axis=0, concat_axis=0, tiled=T...  59.9 us
    all_to_all x1, waiting for transfers between devices, local(): lax.all_to_all(expert_out, 'expert', split_axis=0, concat_axis=0, tiled=T...  40.8 us
    all_to_all x1, waiting for transfers between devices, local(): lax.all_to_all(send_grads, 'expert', split_axis=0, concat_axis=0, tiled=T...  39.1 us
    all_to_all x1, waiting for transfers between devices, local(): lax.all_to_all(send_rows, 'expert', split_axis=0, concat_axis=0, tiled=True)  35.7 us
    psum x2, waiting for transfers between devices, local(): router_grad = lax.psum(lax.psum(router_term, 'expert'), 'dp')  24.3 us
    all_to_all x1, starting transfers between devices, local(): lax.all_to_all(expert_out, 'expert', split_axis=0, concat_axis=0, tiled=T...  11.3 us
  transfers between devices with their start and end apart: 8, of which 7 were waited for; matrix products, arithmetic and copies ran while one was open for 11% of the time, Pallas kernels for 0%

profile of v1, /device:TPU:0, one launch (start us, length us, event | category | flops | bytes accessed | tf_op | source)
XLA Modules:
  0.0 473.9 jit_solution(11631644277656374392)
XLA Ops:
  8.9 1.1 fusion.55
  12.9 4.0 convolution_convert_fusion
  16.9 7.5 %all-to-all-start.2 = ((bf16[16,1,32,2048]{3,2,1,0:T(8,128)(2,1)}), bf16[16,1,32,2048]{3,2,1,0:T(8,128)(2,1)}, u32[]{:S(2)}, u32[]{:S(2)}) async-start(bf16[16,1,32,2048]{3,2,1,0:T(8,128)(2,1)} %bitcast.171), calls=%async_computation.2 | async-start | bytes 4194304 | tf_op jit(solution)/shard_map/all_to_all | solution.py:86
  24.5 2.1 convolution_convert_fusion.1
  26.6 39.1 %all-to-all-done.2 = bf16[16,1,32,2048]{3,2,1,0:T(8,128)(2,1)} async-done(((bf16[16,1,32,2048]{3,2,1,0:T(8,128)(2,1)}), bf16[16,1,32,2048]{3,2,1,0:T(8,128)(2,1)}, u32[]{:S(2)}, u32[]{:S(2)}) %all-to-all-start.2) | async-done | bytes 2097184 | tf_op jit(solution)/shard_map/all_to_all | solution.py:86
  65.7 11.3 %all-to-all-start = ((bf16[16,1,32,2048]{3,2,1,0:T(8,128)(2,1)}), bf16[16,1,32,2048]{3,2,1,0:T(8,128)(2,1)}, u32[]{:S(2)}, u32[]{:S(2)}) async-start(bf16[16,1,32,2048]{3,2,1,0:T(8,128)(2,1)} %bitcast.170), calls=%async_computation | async-start | bytes 4194304 | tf_op jit(solution)/shard_map/all_to_all | solution.py:83
  76.9 5.5 %fusion = f32[16,32,768]{2,1,0:T(8,128)} fusion(bf16[1,768,2048]{2,1,0:T(8,128)(2,1)} %param.15, bf16[16,1,32,2048]{3,2,1,0:T(8,128)(2,1)} %all-to-all-done.2), kind=kOutput, calls=%fused_computation.6 | convolution fusion | flops 1610612736 | bytes 6815744 | tf_op jit(solution)/shard_map/sjcd,jfd->sjcf/dot_general | solution.py:29
  82.4 35.7 %all-to-all-done = bf16[16,1,32,2048]{3,2,1,0:T(8,128)(2,1)} async-done(((bf16[16,1,32,2048]{3,2,1,0:T(8,128)(2,1)}), bf16[16,1,32,2048]{3,2,1,0:T(8,128)(2,1)}, u32[]{:S(2)}, u32[]{:S(2)}) %all-to-all-start) | async-done | bytes 2097184 | tf_op jit(solution)/shard_map/all_to_all | solution.py:83
  118.1 4.4 fusion.6
  122.6 5.2 %fusion.41 = (bf16[16,32,768]{2,1,0:T(8,128)(2,1)S(1)}, bf16[16,1,32,768]{3,2,0,1:T(8,128)(2,1)}, bf16[16,32,768]{2,1,0:T(8,128)(2,1)}) fusion(f32[16,32,768]{2,1,0:T(8,128)S(1)} %fusion.6, f32[16,32,768]{2,1,0:T(8,128)S(1)} %copy-done.7, bf16[1,2048,768]{2,1,0:T(8,128)(2,1)S(1)} %copy-done, bf16[16,1,32,2048]{3,2,1,0:T(8,128)(2,1)} %all-to-all-done), kind=kOutput, calls=%fused_computation.53 | convolution fusion | flops 1616510976 | bytes 10747904 | tf_op jit(solution)/shard_map/sjcd,jdf->sjcf/dot_general | solution.py:15
  128.7 3.1 fusion.17
  131.8 11.3 %all-to-all-start.1 = ((bf16[16,1,32,2048]{3,2,1,0:T(8,128)(2,1)}), bf16[16,1,32,2048]{3,2,1,0:T(8,128)(2,1)}, u32[]{:S(2)}, u32[]{:S(2)}) async-start(bf16[16,1,32,2048]{3,2,1,0:T(8,128)(2,1)} %fusion.17), calls=%async_computation.1 | async-start | bytes 4194304 | tf_op jit(solution)/shard_map/all_to_all | solution.py:85
  143.4 40.8 %all-to-all-done.1 = bf16[16,1,32,2048]{3,2,1,0:T(8,128)(2,1)} async-done(((bf16[16,1,32,2048]{3,2,1,0:T(8,128)(2,1)}), bf16[16,1,32,2048]{3,2,1,0:T(8,128)(2,1)}, u32[]{:S(2)}, u32[]{:S(2)}) %all-to-all-start.1) | async-done | bytes 2097184 | tf_op jit(solution)/shard_map/all_to_all | solution.py:85
  184.3 5.2 %gather_fusion = bf16[256,2048]{1,0:T(8,128)(2,1)} fusion(bf16[512,2048]{1,0:T(8,128)(2,1)} %bitcast.22, s32[1024]{0:T(1024)S(1)} %pad_clamp_fusion), kind=kCustom, calls=%fused_computation.clone | custom fusion | bytes 2098176 | tf_op jit(solution)/shard_map/jit(_take)/gather | solution.py:106
  189.5 2.2 fusion.39
  192.8 6.3 %convolution_bitcast_fusion = f32[1,768,2048]{2,1,0:T(8,128)} fusion(bf16[16,32,768]{2,1,0:T(8,128)(2,1)} %copy-done.8, bf16[16,1,32,2048]{3,2,1,0:T(8,128)(2,1)} %all-to-all-done.2), kind=kOutput, calls=%fused_computation.3 | convolution fusion | flops 1610612736 | bytes 9175040 | tf_op jit(solution)/shard_map/sjcf,sjcd->jfd/dot_general | solution.py:94
  199.2 6.3 %convolution_bitcast_fusion.2 = f32[1,2048,768]{2,1,0:T(8,128)} fusion(bf16[16,1,32,2048]{3,2,1,0:T(8,128)(2,1)} %all-to-all-done, bf16[16,1,32,768]{3,2,0,1:T(8,128)(2,1)} %get-tuple-element.14), kind=kOutput, calls=%fused_computation.5 | convolution fusion | flops 1610612736 | bytes 9175040 | tf_op jit(solution)/shard_map/sjcd,sjcf->jdf/dot_general | solution.py:92
  205.5 6.2 %convolution_bitcast_fusion.1 = f32[1,2048,768]{2,1,0:T(8,128)} fusion(bf16[16,32,768]{2,1,0:T(8,128)(2,1)} %get-tuple-element.15, bf16[16,1,32,2048]{3,2,1,0:T(8,128)(2,1)} %all-to-all-done), kind=kOutput, calls=%fused_computation.4 | convolution fusion | flops 1610612736 | bytes 9175040 | tf_op jit(solution)/shard_map/sjcd,sjcf->jdf/dot_general | solution.py:93
  211.8 4.4 fusion.4
  216.3 1.8 fusion.20
  218.1 59.9 %all_to_all.20 = bf16[16,1,32,2048]{3,2,1,0:T(8,128)(2,1)} all-to-all(bf16[16,1,32,2048]{3,2,1,0:T(8,128)(2,1)S(1)} %fusion.20), channel_id=1, replica_groups=mesh['dp'=2,'expert'=16] {'expert'}, dimensions={0} | all-to-all | bytes 4194304 | tf_op jit(solution)/shard_map/all_to_all | solution.py:90
  278.0 5.2 %gather_fusion.1 = bf16[256,2048]{1,0:T(8,128)(2,1)} fusion(bf16[512,2048]{1,0:T(8,128)(2,1)} %bitcast.169, s32[1024]{0:T(1024)S(1)} %pad_clamp_fusion), kind=kCustom, calls=%fused_computation.1.clone | custom fusion | bytes 2098176 | tf_op jit(solution)/shard_map/jit(_take)/gather | solution.py:109
  283.2 3.9 convert_reduce_fusion
  287.1 3.9 all-reduce.3.cloned.1.call-done
  291.1 1.0 fusion.23
  292.1 3.4 convert_element_type.102
  295.4 66.6 %reduce-scatter.4.cloned.1.call-done = f32[1,1024,768]{2,1,0:T(8,128)} async-done(((f32[1,2048,768]{2,1,0:T(8,128)}), f32[1,1024,768]{2,1,0:T(8,128)}) %reduce-scatter.4.cloned.1.call-update) | async-done | bytes 3145744 | tf_op jit(solution)/shard_map/reduce_scatter | solution.py:98
  362.0 3.2 convert_element_type.100
  365.2 76.0 %reduce-scatter.6.cloned.1.call-done = f32[1,1024,768]{2,1,0:T(8,128)} async-done(((f32[1,2048,768]{2,1,0:T(8,128)}), f32[1,1024,768]{2,1,0:T(8,128)}) %reduce-scatter.6.cloned.1.call-update) | async-done | bytes 3145744 | tf_op jit(solution)/shard_map/reduce_scatter | solution.py:99
  441.2 3.2 convert_element_type.101
  444.4 20.4 %all-reduce.5.cloned.1.call-done = f32[2048,16]{0,1:T(8,128)} async-done(((f32[2048,16]{0,1:T(8,128)}), f32[2048,16]{0,1:T(8,128)}) %all-reduce.5.cloned.1.call-update) | async-done | bytes 131088 | tf_op jit(solution)/shard_map/psum | solution.py:122
  464.7 1.6 copy.45
  (52 shorter events, 6.3 us)
Async XLA Ops:
  8.0 114.5 %copy-start = (bf16[1,2048,768]{2,1,0:T(8,128)(2,1)S(1)}, bf16[1,2048,768]{2,1,0:T(8,128)(2,1)}, u32[]{:S(2)}) copy-start(bf16[1,2048,768]{2,1,0:T(8,128)(2,1)} %param.13) | copy-start | bytes 9437188
  16.9 7.6 %copy-start.1 = (bf16[32,2048]{1,0:T(8,128)(2,1)S(1)}, bf16[32,2048]{1,0:T(8,128)(2,1)}, u32[]{:S(2)}) copy-start(bf16[32,2048]{1,0:T(8,128)(2,1)} %param.9) | copy-start | bytes 393220
  16.9 48.7 %all-to-all-start.2 = ((bf16[16,1,32,2048]{3,2,1,0:T(8,128)(2,1)}), bf16[16,1,32,2048]{3,2,1,0:T(8,128)(2,1)}, u32[]{:S(2)}, u32[]{:S(2)}) async-start(bf16[16,1,32,2048]{3,2,1,0:T(8,128)(2,1)} %bitcast.171), calls=%async_computation.2 | async-start | bytes 4194304 | tf_op jit(solution)/shard_map/all_to_all | solution.py:86
  65.7 52.4 %all-to-all-start = ((bf16[16,1,32,2048]{3,2,1,0:T(8,128)(2,1)}), bf16[16,1,32,2048]{3,2,1,0:T(8,128)(2,1)}, u32[]{:S(2)}, u32[]{:S(2)}) async-start(bf16[16,1,32,2048]{3,2,1,0:T(8,128)(2,1)} %bitcast.170), calls=%async_computation | async-start | bytes 4194304 | tf_op jit(solution)/shard_map/all_to_all | solution.py:83
  118.1 4.4 copy-start.7
  122.5 6.2 %copy-start.5 = (bf16[1,768,2048]{2,1,0:T(8,128)(2,1)S(1)}, bf16[1,768,2048]{2,1,0:T(8,128)(2,1)}, u32[]{:S(2)}) copy-start(bf16[1,768,2048]{2,1,0:T(8,128)(2,1)} %param.15) | copy-start | bytes 9437188
  127.8 0.9 copy-start.8
  131.8 52.4 %all-to-all-start.1 = ((bf16[16,1,32,2048]{3,2,1,0:T(8,128)(2,1)}), bf16[16,1,32,2048]{3,2,1,0:T(8,128)(2,1)}, u32[]{:S(2)}, u32[]{:S(2)}) async-start(bf16[16,1,32,2048]{3,2,1,0:T(8,128)(2,1)} %fusion.17), calls=%async_computation.1 | async-start | bytes 4194304 | tf_op jit(solution)/shard_map/all_to_all | solution.py:85
  143.1 148.0 %all-reduce.3.cloned.1.call-start = ((), (), s32[]{:S(2)}) async-start(), calls=%async_computation.10 | async-start | bytes 262144 | tf_op jit(solution)/shard_map/psum | solution.py:122
  184.3 5.2 %copy-start.3 = (bf16[32,2048]{1,0:T(8,128)(2,1)S(1)}, bf16[32,2048]{1,0:T(8,128)(2,1)}, u32[]{:S(2)}) copy-start(bf16[32,2048]{1,0:T(8,128)(2,1)} %param.11) | copy-start | bytes 393220
  189.5 2.3 copy-start.4
  192.7 99.4 %reduce-scatter.8.cloned.1.call-start = ((), (), s32[]{:S(2)}) async-start(), calls=%async_computation.9 | async-start | bytes 9437184 | tf_op jit(solution)/shard_map/reduce_scatter | solution.py:100
  199.1 162.9 %reduce-scatter.4.cloned.1.call-start = ((), (), s32[]{:S(2)}) async-start(), calls=%async_computation.7 | async-start | bytes 9437184 | tf_op jit(solution)/shard_map/reduce_scatter | solution.py:98
  205.4 235.7 %reduce-scatter.6.cloned.1.call-start = ((), (), s32[]{:S(2)}) async-start(), calls=%async_computation.8 | async-start | bytes 9437184 | tf_op jit(solution)/shard_map/reduce_scatter | solution.py:99
  211.7 253.0 %all-reduce.5.cloned.1.call-start = ((), (), s32[]{:S(2)}) async-start(), calls=%async_computation.11 | async-start | bytes 262144 | tf_op jit(solution)/shard_map/psum | solution.py:122
  211.8 4.5 copy-start.6
  283.2 7.9 %copy-start.2 = (bf16[2048,16]{0,1:T(8,128)(2,1)S(1)}, bf16[2048,16]{0,1:T(8,128)(2,1)}, u32[]{:S(2)}) copy-start(bf16[2048,16]{0,1:T(8,128)(2,1)} %param.12) | copy-start | bytes 196612
Sparse Core Ops, SparseCore 0:
  192.8 98.1 all-reduce.2
Sparse Core Ops, SparseCore 1:
  199.2 83.5 reduce-scatter.7
  285.0 77.0 reduce-scatter.3
  364.2 76.9 reduce-scatter.5
  443.5 21.1 all-reduce.4
